TPU v7x, 128 devices: a whole 4x4x4 slice. The times are simulated.
128 devices in a mesh: stu: 8 (over y, core), tea: 16 (over z, x).
Axes of the slice: x: 4, y: 4, z: 4, core: 2. Of those that a mesh axis runs over, the one named last changes fastest.
Arguments:
- student: bfloat16 [16384, 2048], P('stu', 'tea'), may hold values from -8 to 8
- teacher: bfloat16 [16384, 2048], P('tea', 'stu'), may hold values from -8 to 8
- band_start: int32 [32], replicated, may hold values from 0 to 28, as said below
Outputs:
- grad_student: float32 [16384, 2048], P('stu', 'tea')
- stu_pot: float32 [16384], P('stu')
- tea_pot: float32 [16384], P('tea')
- loss: float32 [], replicated
Inputs may be any that keep to these rules, and one draw needn't show every extreme that they name: student block a is paired with teacher blocks band_start[a] to band_start[a] + 3; every teacher block is paired with at least one student block, block 0 with student block 0.
All inputs are finite; a program needn't handle non-finite values.
Results may differ from a plain program's by a relative error of at most 0.002.
Values may be sent and summed in bfloat16 or wider, within the bound.
A program may use at most 192 MiB of HBM per device.

v0:
```python
import math

import jax
import jax.numpy as jnp
from jax import lax
from jax.sharding import PartitionSpec as P

D = 2048
BLK = 512
W = 4
ITERS = 3


epsilon = 0.02
masked_score = -1e30


def squares(rows):
    return jnp.sum(jnp.square(rows.astype(jnp.float32)), axis=1)


def row_logsum(scores, listed):
    highest = lax.pmax(jnp.max(scores, axis=1), "tea")
    local_total = jnp.sum(jnp.where(listed, jnp.exp(scores - highest[:, None]), 0.0), axis=1)
    summed = lax.psum(local_total, "tea")
    return highest + jnp.log(summed)


def col_logsum(scores, listed):
    highest = lax.pmax(jnp.max(scores, axis=0), "stu")
    local_total = jnp.sum(jnp.where(listed, jnp.exp(scores - highest[None, :]), 0.0), axis=0)
    summed = lax.psum(local_total, "stu")
    return highest + jnp.log(summed)


def local(student, teacher, band_start):
    stu_rows = student.shape[0]
    tea_rows = teacher.shape[0]
    token_total = stu_rows * lax.axis_size("stu")
    first_stu = lax.axis_index("stu") * stu_rows
    first_tea = lax.axis_index("tea") * tea_rows
    stu_block = (first_stu + jnp.arange(stu_rows, dtype=jnp.int32)) // BLK
    tea_block = (first_tea + jnp.arange(tea_rows, dtype=jnp.int32)) // BLK
    matches = stu_block[:, None] == jnp.arange(band_start.shape[0], dtype=jnp.int32)[None, :]
    lowest = jnp.sum(jnp.where(matches, band_start[None, :], 0), axis=1)
    listed = (tea_block[None, :] >= lowest[:, None]) & (tea_block[None, :] < lowest[:, None] + W)
    active = jnp.any(listed)
    student_full = lax.all_gather(student, "tea", axis=1, tiled=True)
    teacher_full = lax.all_gather(teacher, "stu", axis=1, tiled=True)

    def inner_tile(operands):
        return lax.dot_general(
            operands[0], operands[1], (((1,), (1,)), ((), ())), preferred_element_type=jnp.float32
        )

    def empty_tile(operands):
        return jnp.zeros((stu_rows, tea_rows), jnp.float32)

    inner = lax.cond(active, inner_tile, empty_tile, (student_full, teacher_full))
    tile_cost = (squares(student_full)[:, None] + squares(teacher_full)[None, :] - 2.0 * inner) / D
    log_marginal = -math.log(token_total)
    tea_pot = jnp.zeros((tea_rows,), jnp.float32)
    stu_pot = jnp.zeros((stu_rows,), jnp.float32)
    for sweep in range(ITERS):
        scores = jnp.where(listed, (tea_pot[None, :] - tile_cost) / epsilon, masked_score)
        stu_pot = epsilon * log_marginal - epsilon * row_logsum(scores, listed)
        scores = jnp.where(listed, (stu_pot[:, None] - tile_cost) / epsilon, masked_score)
        tea_pot = epsilon * log_marginal - epsilon * col_logsum(scores, listed)
    transport = jnp.where(
        listed, jnp.exp((stu_pot[:, None] + tea_pot[None, :] - tile_cost) / epsilon), 0.0
    )
    loss = lax.psum(jnp.sum(transport * tile_cost), ("stu", "tea"))
    weights = (transport * token_total).astype(jnp.bfloat16)
    row_mass = jnp.sum(weights.astype(jnp.float32), axis=1)

    def pull_tile(operands):
        return jnp.dot(operands[0], operands[1], preferred_element_type=jnp.float32)

    def empty_pull(operands):
        return jnp.zeros((stu_rows, operands[1].shape[1]), jnp.float32)

    pulled = lax.cond(active, pull_tile, empty_pull, (weights, teacher_full))
    partial_terms = row_mass[:, None] * student_full.astype(jnp.float32) - pulled
    grad_student = lax.psum_scatter(partial_terms, "tea", scatter_dimension=1, tiled=True)
    return (grad_student, stu_pot, tea_pot, loss)


def solution(mesh):
    placed = (P("stu", "tea"), P("tea", "stu"), P())
    return jax.shard_map(
        local,
        mesh=mesh,
        in_specs=placed,
        out_specs=(P("stu", "tea"), P("stu"), P("tea"), P()),
        check_vma=False,
    )
```

profile of v0, /device:TPU:1, one launch (start us, length us, event | category | flops | bytes accessed | tf_op | source)
XLA Modules:
  0.0 676.5 jit_solution(12704990563506161459)
XLA Ops:
  13.0 36.4 %all-gather.5.cloned.1.call-done = bf16[1024,2048]{1,0:T(8,128)(2,1)} async-done(((bf16[1024,256]{1,0:T(8,128)(2,1)}), bf16[1024,2048]{1,0:T(8,128)(2,1)}) %all-gather.5.cloned.1.call-update) | async-done | bytes 4194320 | tf_op jit(solution)/shard_map/all_gather | solution.py:49
  52.5 77.2 %all-gather.3.cloned.1.call-done = bf16[2048,2048]{1,0:T(8,128)(2,1)} async-done(((bf16[2048,128]{1,0:T(8,128)(2,1)}), bf16[2048,2048]{1,0:T(8,128)(2,1)}) %all-gather.3.cloned.1.call-update) | async-done | bytes 8388624 | tf_op jit(solution)/shard_map/all_gather | solution.py:48
  143.7 37.4 %pmax.42 = f32[2048]{0:T(1024)S(1)} all-reduce(f32[2048]{0:T(1024)S(1)} %fusion.2), channel_id=1, replica_groups=mesh['stu'=8,'tea'=16] {'tea'}, use_global_device_ids=true, to_apply=%region_7.8 | all-reduce | flops 2048 | bytes 16384 | tf_op jit(solution)/shard_map/pmax | solution.py:23
  187.8 29.0 %psum.49 = f32[2048]{0:T(1024)S(1)} all-reduce(f32[2048]{0:T(1024)S(1)} %select_reduce_fusion.5), channel_id=1, replica_groups=mesh['stu'=8,'tea'=16] {'tea'}, use_global_device_ids=true, to_apply=%region_9.10 | all-reduce | flops 2048 | bytes 16384 | tf_op jit(solution)/shard_map/psum | solution.py:25
  222.8 31.2 %pmax.43 = f32[1024]{0:T(1024)S(1)} all-reduce(f32[1024]{0:T(1024)S(1)} %fusion.3), channel_id=1, replica_groups=mesh['stu'=8,'tea'=16] {'stu'}, use_global_device_ids=true, to_apply=%region_11.12 | all-reduce | flops 1024 | bytes 8192 | tf_op jit(solution)/shard_map/pmax | solution.py:30
  254.0 7.2 %select_reduce_fusion.4 = f32[1024]{0:T(1024)S(1)} fusion(f32[1024]{0:T(1024)S(1)} %pmax.43, f32[2048]{0:T(1024)S(1)} %multiply_subtract_fusion.2, f32[2048,1024]{1,0:T(8,128)} %get-tuple-element.25, f32[1024]{0:T(1024)S(1)} %multiply_reduce_fusion.1, f32[2048]{0:T(1024)S(1)} %fusion, s32[2048]{0:T(1024)S(1)} %broadcast_add_fusion, ...), kind=kLoop, calls=%fused_computation.16 | loop fusion | flops 27261952 | bytes 8437760 | tf_op jit(solution)/shard_map/reduce_sum | solution.py:31
  261.2 12.4 %psum.50 = f32[1024]{0:T(1024)S(1)} all-reduce(f32[1024]{0:T(1024)S(1)} %select_reduce_fusion.4), channel_id=1, replica_groups=mesh['stu'=8,'tea'=16] {'stu'}, use_global_device_ids=true, to_apply=%region_13.14 | all-reduce | flops 1024 | bytes 8192 | tf_op jit(solution)/shard_map/psum | solution.py:32
  279.9 30.2 %pmax.44 = f32[2048]{0:T(1024)S(1)} all-reduce(f32[2048]{0:T(1024)S(1)} %fusion.4), channel_id=1, replica_groups=mesh['stu'=8,'tea'=16] {'tea'}, use_global_device_ids=true, to_apply=%region_15.16 | all-reduce | flops 2048 | bytes 16384 | tf_op jit(solution)/shard_map/pmax | solution.py:23
  310.1 6.8 %select_reduce_fusion.3 = f32[2048]{0:T(1024)S(1)} fusion(f32[2048]{0:T(1024)S(1)} %pmax.44, f32[1024]{0:T(1024)S(1)} %multiply_subtract_fusion.5, f32[2048,1024]{1,0:T(8,128)} %get-tuple-element.25, f32[1024]{0:T(1024)S(1)} %multiply_reduce_fusion.1, f32[2048]{0:T(1024)S(1)} %fusion, s32[2048]{0:T(1024)S(1)} %broadcast_add_fusion, ...), kind=kLoop, calls=%fused_computation.14 | loop fusion | flops 27260928 | bytes 8441856 | tf_op jit(solution)/shard_map/reduce_sum | solution.py:24
  316.9 29.4 %psum.51 = f32[2048]{0:T(1024)S(1)} all-reduce(f32[2048]{0:T(1024)S(1)} %select_reduce_fusion.3), channel_id=1, replica_groups=mesh['stu'=8,'tea'=16] {'tea'}, use_global_device_ids=true, to_apply=%region_17.18 | all-reduce | flops 2048 | bytes 16384 | tf_op jit(solution)/shard_map/psum | solution.py:25
  352.2 26.8 %pmax.45 = f32[1024]{0:T(1024)S(1)} all-reduce(f32[1024]{0:T(1024)S(1)} %fusion.5), channel_id=1, replica_groups=mesh['stu'=8,'tea'=16] {'stu'}, use_global_device_ids=true, to_apply=%region_19.20 | all-reduce | flops 1024 | bytes 8192 | tf_op jit(solution)/shard_map/pmax | solution.py:30
  379.0 7.2 %select_reduce_fusion.2 = f32[1024]{0:T(1024)S(1)} fusion(f32[1024]{0:T(1024)S(1)} %pmax.45, f32[2048]{0:T(1024)S(1)} %multiply_subtract_fusion.1, f32[2048,1024]{1,0:T(8,128)} %get-tuple-element.25, f32[1024]{0:T(1024)S(1)} %multiply_reduce_fusion.1, f32[2048]{0:T(1024)S(1)} %fusion, s32[2048]{0:T(1024)S(1)} %broadcast_add_fusion, ...), kind=kLoop, calls=%fused_computation.12 | loop fusion | flops 27261952 | bytes 8437760 | tf_op jit(solution)/shard_map/reduce_sum | solution.py:31
  386.2 12.4 %psum.52 = f32[1024]{0:T(1024)S(1)} all-reduce(f32[1024]{0:T(1024)S(1)} %select_reduce_fusion.2), channel_id=1, replica_groups=mesh['stu'=8,'tea'=16] {'stu'}, use_global_device_ids=true, to_apply=%region_21.22 | all-reduce | flops 1024 | bytes 8192 | tf_op jit(solution)/shard_map/psum | solution.py:32
  404.9 29.8 %pmax.46 = f32[2048]{0:T(1024)S(1)} all-reduce(f32[2048]{0:T(1024)S(1)} %fusion.6), channel_id=1, replica_groups=mesh['stu'=8,'tea'=16] {'tea'}, use_global_device_ids=true, to_apply=%region_23.24 | all-reduce | flops 2048 | bytes 16384 | tf_op jit(solution)/shard_map/pmax | solution.py:23
  441.6 29.7 %psum.53 = f32[2048]{0:T(1024)S(1)} all-reduce(f32[2048]{0:T(1024)S(1)} %select_reduce_fusion.1), channel_id=1, replica_groups=mesh['stu'=8,'tea'=16] {'tea'}, use_global_device_ids=true, to_apply=%region_25.26 | all-reduce | flops 2048 | bytes 16384 | tf_op jit(solution)/shard_map/psum | solution.py:25
  477.2 26.8 %pmax.47 = f32[1024]{0:T(1024)S(1)} all-reduce(f32[1024]{0:T(1024)S(1)} %fusion.7), channel_id=1, replica_groups=mesh['stu'=8,'tea'=16] {'stu'}, use_global_device_ids=true, to_apply=%region_27.28 | all-reduce | flops 1024 | bytes 8192 | tf_op jit(solution)/shard_map/pmax | solution.py:30
  504.0 7.2 %select_reduce_fusion = f32[1024]{0:T(1024)S(1)} fusion(f32[1024]{0:T(1024)S(1)} %pmax.47, f32[2048]{0:T(1024)S(1)} %multiply_subtract_fusion, f32[2048,1024]{1,0:T(8,128)} %get-tuple-element.25, f32[1024]{0:T(1024)S(1)} %multiply_reduce_fusion.1, f32[2048]{0:T(1024)S(1)} %fusion, s32[2048]{0:T(1024)S(1)} %broadcast_add_fusion, ...), kind=kLoop, calls=%fused_computation.8 | loop fusion | flops 27261952 | bytes 8437760 | tf_op jit(solution)/shard_map/reduce_sum | solution.py:31
  511.2 12.6 %psum.54 = f32[1024]{0:T(1024)S(1)} all-reduce(f32[1024]{0:T(1024)S(1)} %select_reduce_fusion), channel_id=1, replica_groups=mesh['stu'=8,'tea'=16] {'stu'}, use_global_device_ids=true, to_apply=%region_29.30 | all-reduce | flops 1024 | bytes 8192 | tf_op jit(solution)/shard_map/psum | solution.py:32
  523.9 10.9 %convert_reduce_fusion = (f32[2048]{0:T(1024)S(1)}, bf16[2048,1024]{1,0:T(8,128)(2,1)}, f32[]{:T(128)}) fusion(f32[2048,1024]{1,0:T(8,128)} %get-tuple-element.25, f32[1024]{0:T(1024)S(1)} %multiply_reduce_fusion.1, f32[2048]{0:T(1024)S(1)} %fusion, f32[1024]{0:T(1024)S(1)} %multiply_subtract_fusion.3, f32[2048]{0:T(1024)S(1)} %multiply_subtract_fusion, ...), kind=kLoop, calls=%fused_computation.5 | loop fusion | flops 35649536 | bytes 12636164 | tf_op jit(solution)/shard_map/reduce_sum | solution.py:74
  534.8 7.8 %conditional.3 = (f32[2048,2048]{1,0:T(8,128)}) conditional(s32[]{:T(128)} %convert_element_type.19, () %tuple.22, (bf16[2048,1024]{1,0:T(8,128)(2,1)}, bf16[1024,2048]{1,0:T(8,128)(2,1)}) %tuple.23), branch_computations={%region_31.32_spmd, %region_32.33_spmd} | conditional | flops 8589934592 | bytes 25165832 | solution.py:82
  534.8 7.8 %broadcast.117 = f32[2048,2048]{1,0:T(8,128)} broadcast(f32[]{:T(128)} %constant.54.clone), dimensions={} | broadcast | bytes 16777220 | tf_op jit(solution)/shard_map/broadcast.9
  542.6 13.9 %fusion.1 = f32[2048,2048]{1,0:T(8,128)} fusion(f32[2048,2048]{1,0:T(8,128)} %get-tuple-element.26, bf16[2048,2048]{1,0:T(8,128)(2,1)} %all-gather.3.cloned.1.call-done, f32[2048]{0:T(1024)S(1)} %get-tuple-element.22), kind=kLoop, calls=%fused_computation.3 | loop fusion | flops 12582912 | bytes 41951232 | tf_op jit(solution)/shard_map/sub | solution.py:83
  556.6 71.6 %psum.55 = f32[]{:T(128)} all-reduce(f32[]{:T(128)} %get-tuple-element.24), channel_id=1, replica_groups=mesh['stu'=8,'tea'=16] {'stu','tea'}, use_global_device_ids=true, to_apply=%region_35.36 | all-reduce | flops 1 | bytes 8 | tf_op jit(solution)/shard_map/psum | solution.py:72
  628.2 41.8 %reduce-scatter.2.cloned.1.call-done = f32[2048,128]{1,0:T(8,128)} async-done(((f32[2048,2048]{1,0:T(8,128)}), f32[2048,128]{1,0:T(8,128)}) %reduce-scatter.2.cloned.1.call-update) | async-done | bytes 1048592 | tf_op jit(solution)/shard_map/reduce_scatter | solution.py:84
  (35 shorter events, 70.1 us)
Async XLA Ops:
  7.2 42.3 %all-gather.5.cloned.1.call-start = ((), (), s32[]{:S(2)}) async-start(), calls=%async_computation.2 | async-start | bytes 4718592 | tf_op jit(solution)/shard_map/all_gather | solution.py:49
  7.9 121.8 %all-gather.3.cloned.1.call-start = ((), (), s32[]{:S(2)}) async-start(), calls=%async_computation.1 | async-start | bytes 8912896 | tf_op jit(solution)/shard_map/all_gather | solution.py:48
  8.6 661.3 %reduce-scatter.2.cloned.1.call-start = ((), (), s32[]{:S(2)}) async-start(), calls=%async_computation.3 | async-start | bytes 17825792 | tf_op jit(solution)/shard_map/reduce_scatter | solution.py:84
  134.0 5.8 copy-start
  471.3 52.5 %copy-start.1 = (f32[2048]{0:T(1024)}, f32[2048]{0:T(1024)S(1)}, u32[]{:S(2)}) copy-start(f32[2048]{0:T(1024)S(1)} %multiply_subtract_fusion) | copy-start | bytes 24580
  523.9 10.9 %copy-start.2 = (f32[1024]{0:T(1024)}, f32[1024]{0:T(1024)S(1)}, u32[]{:S(2)}) copy-start(f32[1024]{0:T(1024)S(1)} %multiply_subtract_fusion.3) | copy-start | bytes 12292
Sparse Core Ops, SparseCore 0:
  9.7 39.6 all-gather.4
  51.5 78.1 all-gather.2
  556.7 113.2 reduce-scatter.1
where the time goes:
time: 677 us; the launch traced here: 676 us
  blocking collectives  380 us (56%)
  waiting for transfers between devices  157 us (23%)
  other arithmetic  113 us (17%)
  between operations  14.6 us (2%)
  local copies, waits for them, and re-layouts  12.7 us (2%)
    pmax x3, blocking collectives, row_logsum(): highest = lax.pmax(jnp.max(scores, axis=1), 'tea')  97.5 us
    psum x3, blocking collectives, row_logsum(): summed = lax.psum(local_total, 'tea')  88.2 us
    pmax x3, blocking collectives, col_logsum(): highest = lax.pmax(jnp.max(scores, axis=0), 'stu')  84.8 us
    all_gather x1, waiting for transfers between devices, local(): student_full = lax.all_gather(student, 'tea', axis=1, tiled=True)  77.2 us
    psum x1, blocking collectives, local(): loss = lax.psum(jnp.sum(transport * tile_cost), ('stu', 'tea'))  71.6 us
    reduce_scatter x1, waiting for transfers between devices, local(): lax.psum_scatter(partial_terms, 'tea', scatter_dimension=1, tiled=True)  41.8 us
    psum x3, blocking collectives, col_logsum(): summed = lax.psum(local_total, 'stu')  37.5 us
    all_gather x1, waiting for transfers between devices, local(): teacher_full = lax.all_gather(teacher, 'stu', axis=1, tiled=True)  36.4 us
  transfers between devices with their start and end apart: 3, of which 3 were waited for; matrix products, arithmetic and copies ran while one was open for 1% of the time, Pallas kernels for 0%

commit v1 on v0

v1 whole, which is shorter than its diff:
```python
import functools
import math

import jax
import jax.numpy as jnp
from jax import lax
from jax.experimental import pallas as pl
from jax.experimental.pallas import tpu as pltpu
from jax.sharding import PartitionSpec as P

D = 2048
BLK = 512
W = 4
ITERS = 3
LANES = 128
ROWS = 2048
COLS = 1024
HALF = ROWS // 2
QUARTER = ROWS // 4
TILES = COLS // LANES
LINES = ROWS // LANES
TOKENS = 16384

epsilon = 0.02
kappa = math.log2(math.e) / epsilon
log2e = math.log2(math.e)
log2_tokens = math.log2(TOKENS)
unlisted = -1e30
MESH = pl.DeviceIdType.MESH
f32 = jnp.float32
bf16 = jnp.bfloat16


def aligned(start, size):
    return pl.ds(pl.multiple_of(start, size), size)


def diagonal():
    rows = lax.broadcasted_iota(jnp.int32, (LANES, LANES), 0)
    cols = lax.broadcasted_iota(jnp.int32, (LANES, LANES), 1)
    return rows == cols


def to_lanes(column):
    return jnp.sum(jnp.where(diagonal(), column, 0.0), axis=0, keepdims=True)


def to_sublanes(row):
    return jnp.sum(jnp.where(diagonal(), row, 0.0), axis=1, keepdims=True)


def total_of(parts):
    return functools.reduce(lambda a, b: a + b, parts)


def merge(parts):
    highest = functools.reduce(jnp.maximum, [m for m, _ in parts])
    return highest, total_of([s * jnp.exp2(m - highest) for m, s in parts])


class Place:
    def __init__(self):
        self.s = lax.axis_index("stu")
        self.t = lax.axis_index("tea")
        self.y = lax.div(self.s, 2)
        self.core = lax.rem(self.s, 2)
        self.z = lax.div(self.t, 4)
        self.x = lax.rem(self.t, 4)

    def tea(self, dz, dx):
        return lax.rem(self.z + dz, 4) * 4 + lax.rem(self.x + dx, 4)

    def stu(self, dy, dc=0):
        return lax.rem(self.y + dy, 4) * 2 + lax.rem(self.core + dc, 2)

    def at_x(self, d):
        return (self.s, self.tea(0, d))

    def at_z(self, d):
        return (self.s, self.tea(d, 0))

    def at_y(self, d):
        return (self.stu(d), self.t)

    def sibling(self):
        return (self.stu(0, 1), self.t)

    def at_s(self, d):
        return (lax.rem(self.s + d, 8), self.t)


class Wire:
    def __init__(self, send, recv):
        self.send, self.recv, self.used, self.open = send, recv, 0, []

    def start(self, src, dst, device):
        copy = pltpu.make_async_remote_copy(
            src_ref=src, dst_ref=dst,
            send_sem=self.send.at[self.used], recv_sem=self.recv.at[self.used],
            device_id=device, device_id_type=MESH,
        )
        self.used += 1
        copy.start()
        self.open.append(copy)
        return copy

    def drain(self):
        for copy in self.open:
            copy.wait_send()
        self.open = []


WIRES = 200


def gather(me, wire, stu_in, tea_in, S, T, cost_chunk):
    A, B = pl.ds(0, HALF), pl.ds(HALF, HALF)
    quarter = [pl.ds(i * QUARTER, QUARTER) for i in range(4)]

    def piece(dz, dx, rows):
        return S.at[me.tea(dz, dx), rows]

    def push(dz, dx, rows, device):
        return wire.start(piece(dz, dx, rows), piece(dz, dx, rows), device)

    S[me.t] = stu_in[...]
    T[me.s] = tea_in[...]
    up, down = 1, 3
    ax = {up: push(0, 0, A, me.at_x(up)), down: push(0, 0, A, me.at_x(down))}
    bz = {up: push(0, 0, B, me.at_z(up)), down: push(0, 0, B, me.at_z(down))}
    az, bx = {}, {}

    def turn_a(dx):
        for way in (up, down):
            az[dx, way] = push(0, dx, A, me.at_z(way))

    def turn_b(dz):
        for way in (up, down):
            bx[dz, way] = push(dz, 0, B, me.at_x(way))

    turn_a(0)
    turn_b(0)
    t_half = [pl.ds(0, COLS // 2), pl.ds(COLS // 2, COLS // 2)]

    def t_push(dy, dc, rows, device):
        ref = T.at[me.stu(dy, dc), rows]
        return wire.start(ref, ref, device)

    everything = pl.ds(0, COLS)
    ty = {way: t_push(0, 0, everything, me.at_y(way)) for way in (up, down)}
    tc = {0: [t_push(0, 0, everything, me.sibling())]}

    ax_far, bz_far = [], []
    for way, back, keep in ((up, down, 0), (down, up, 1)):
        ax[way].wait_recv()
        ax_far.append(push(0, back, quarter[keep], me.at_x(way)))
        turn_a(back)
        bz[way].wait_recv()
        bz_far.append(push(back, 0, quarter[2 + keep], me.at_z(way)))
        turn_b(back)
    ty_far = []
    for way, back, keep in ((up, down, 0), (down, up, 1)):
        ty[way].wait_recv()
        ty_far.append(t_push(back, 0, t_half[keep], me.at_y(way)))
        tc[back] = [t_push(back, 0, everything, me.sibling())]
    for copy in ax_far:
        copy.wait_recv()
    turn_a(2)
    for copy in bz_far:
        copy.wait_recv()
    turn_b(2)
    tc[2] = []
    for keep, copy in enumerate(ty_far):
        copy.wait_recv()
        tc[2].append(t_push(2, 0, t_half[keep], me.sibling()))

    az_far, bx_far = [], []
    for d in (0, down, up, 2):
        for way, back, keep in ((up, down, 0), (down, up, 1)):
            az[d, way].wait_recv()
            az_far.append(push(back, d, quarter[keep], me.at_z(way)))
            bx[d, way].wait_recv()
            copy = push(d, back, quarter[2 + keep], me.at_x(way))
            bx_far.append((d, copy))
    for dy in (0, down, up, 2):
        for copy in tc[dy]:
            copy.wait_recv()

    def wait_bx(d):
        for at, copy in bx_far:
            if at == d:
                copy.wait_recv()

    for number, dz in enumerate((0, down, up, 2)):
        wait_bx(dz)
        if dz == 2:
            for copy in az_far:
                copy.wait_recv()
        row = lax.rem(me.z + dz, 4)
        cost_chunk(2 * row, number == 0)
        cost_chunk(2 * row + 1, False)


def cost_chunk_of(S, T, z, xsq, ysq):
    def cost_chunk(q, first):
        def rows_block(r, carry):
            rows = aligned(r * 256, 256)
            low, high = S[2 * q, rows, :], S[2 * q + 1, rows, :]
            prod = lax.dot_general(
                jnp.concatenate([low, high], axis=1), T[q],
                (((1,), (1,)), ((), ())), preferred_element_type=f32,
            )
            squared = jnp.square(low.astype(f32)) + jnp.square(high.astype(f32))
            for c in range(TILES):
                tile = prod[:, c * LANES:(c + 1) * LANES]
                z[c, rows, :] = tile if first else z[c, rows, :] + tile
            xsq[rows, :] = squared if first else xsq[rows, :] + squared
            return carry

        lax.fori_loop(0, ROWS // 256, rows_block, 0)

        def cols_block(r, carry):
            rows = aligned(r * LANES, LANES)
            low, high = T[q, rows, :LANES], T[q, rows, LANES:]
            squared = jnp.square(low.astype(f32)) + jnp.square(high.astype(f32))
            ysq[rows, :] = squared if first else ysq[rows, :] + squared
            return carry

        lax.fori_loop(0, TILES, cols_block, 0)

    return cost_chunk


def finish_cost(me, band, z, xsq, ysq, ysq_row):
    for c in range(TILES):
        column = jnp.sum(ysq[c * LANES:(c + 1) * LANES, :], axis=1, keepdims=True)
        ysq_row[:, c * LANES:(c + 1) * LANES] = to_lanes(column)
    scale = kappa / D

    def block(b, carry):
        rows = aligned(b * LANES, LANES)
        total = jnp.broadcast_to(jnp.sum(xsq[rows, :], axis=1, keepdims=True), (LANES, LANES))
        xsq[rows, :] = total
        lowest = jnp.full((LANES, LANES), band[me.s * 4 + lax.div(b, BLK // LANES)], jnp.int32)
        for side in range(2):
            at = jnp.full((LANES, LANES), me.t * 2 + side, jnp.int32)
            listed = (at >= lowest) & (at < lowest + W)
            for c in range(side * 4, side * 4 + 4):
                value = (2.0 * z[c, rows, :] - total - ysq_row[:, c * LANES:(c + 1) * LANES]) * scale
                z[c, rows, :] = jnp.where(listed, value, unlisted)
        return carry

    lax.fori_loop(0, LINES, block, 0)


def row_stats(z, tea, put):
    def block(b, carry):
        highs, sums = [], []
        for part in range(4):
            rows = aligned(b * LANES + part * 32, 32)
            scores = [
                z[c, rows, :] + tea[:, c * LANES:(c + 1) * LANES] for c in range(TILES)
            ]
            high = jnp.max(functools.reduce(jnp.maximum, scores), axis=1, keepdims=True)
            highs.append(high)
            sums.append(
                jnp.sum(total_of([jnp.exp2(v - high) for v in scores]), axis=1, keepdims=True)
            )
        put(
            b,
            to_lanes(jnp.concatenate(highs, axis=0)),
            to_lanes(jnp.concatenate(sums, axis=0)),
        )
        return carry

    lax.fori_loop(0, LINES, block, 0)


def spread_rows(compact, wide):
    def block(b, carry):
        column = to_sublanes(compact[pl.ds(b, 1), :])
        wide[aligned(b * LANES, LANES), :] = jnp.broadcast_to(column, (LANES, LANES))
        return carry

    lax.fori_loop(0, LINES, block, 0)


def col_stats(z, wide, put):
    def block(b, carry):
        rows = aligned(b * LANES, LANES)
        pot = wide[rows, :]
        out = []
        for c in range(TILES):
            high, total = carry[c]
            scores = (z[c, rows, :] + pot).reshape(LANES // 8, 8, LANES)
            new = jnp.maximum(high, jnp.max(scores, axis=0))
            total = total * jnp.exp2(high - new) + jnp.sum(jnp.exp2(scores - new[None]), axis=0)
            out.append((new, total))
        return tuple(out)

    start = tuple(
        (jnp.full((8, LANES), unlisted, f32), jnp.zeros((8, LANES), f32)) for _ in range(TILES)
    )
    done = lax.fori_loop(0, LINES, block, start)
    for c, (high, total) in enumerate(done):
        top = jnp.max(high, axis=0, keepdims=True)
        put(c, top, jnp.sum(total * jnp.exp2(high - top), axis=0, keepdims=True))


def swap(wire, slots, index, count, peer):
    copies = [wire.start(slots.at[index], slots.at[index], peer(d)) for d in range(1, count)]
    for copy in copies:
        copy.wait_recv()


def sweeps(me, wire, z, wide, stu, tea, row_x, row_z, col_s):
    tea[...] = jnp.zeros_like(tea)
    for sweep in range(ITERS):
        rx, rz, cs = row_x.at[sweep], row_z.at[sweep], col_s.at[sweep]

        def put_row(b, high, total):
            rx[me.x, 0, pl.ds(b, 1), :] = high
            rx[me.x, 1, pl.ds(b, 1), :] = total

        row_stats(z, tea, put_row)
        swap(wire, rx, me.x, 4, me.at_x)
        high, total = merge([(rx[i, 0], rx[i, 1]) for i in range(4)])
        rz[me.z, 0] = high
        rz[me.z, 1] = total
        swap(wire, rz, me.z, 4, me.at_z)
        high, total = merge([(rz[i, 0], rz[i, 1]) for i in range(4)])
        stu[...] = -log2_tokens - (high + jnp.log(total) * log2e)
        spread_rows(stu, wide)

        def put_col(c, high, total):
            cs[me.s, 0:1, c * LANES:(c + 1) * LANES] = high
            cs[me.s, 1:2, c * LANES:(c + 1) * LANES] = total

        col_stats(z, wide, put_col)
        swap(wire, cs, me.s, 8, me.at_s)
        high, total = merge([(cs[i, 0:1, :], cs[i, 1:2, :]) for i in range(8)])
        tea[...] = -log2_tokens - (high + jnp.log(total) * log2e)


def make_plan(me, z, wide, tea, xsq, ysq_row, w, sum_x):
    def block(b, loss):
        gammas, betas = [], []
        for part in range(4):
            rows = aligned(b * LANES + part * 32, 32)
            pot = wide[rows, :] + log2_tokens
            mass, pull = [], []
            for c in range(TILES):
                cols = slice(c * LANES, (c + 1) * LANES)
                tile = z[c, rows, :]
                scaled = jnp.exp2(tile + pot + tea[:, cols])
                loss = loss + total_of([(scaled * tile)[8 * i:8 * i + 8] for i in range(4)])
                rounded = scaled.astype(bf16)
                w[rows, cols] = rounded
                rounded = rounded.astype(f32)
                mass.append(rounded)
                pull.append(rounded * (ysq_row[:, cols] + (D / kappa) * tile))
            mass = jnp.sum(total_of(mass), axis=1, keepdims=True)
            pull = jnp.sum(total_of(pull), axis=1, keepdims=True)
            own = xsq[rows, 0:1]
            usable = own > 1e-20
            gamma = jnp.where(usable, 0.5 * (mass + pull / jnp.where(usable, own, 1.0)), 0.0)
            gammas.append(gamma)
            betas.append(mass - gamma)
        wide[aligned(b * LANES, LANES), :] = jnp.broadcast_to(
            jnp.concatenate(gammas, axis=0), (LANES, LANES)
        )
        sum_x[me.x, pl.ds(b, 1), :] = to_lanes(jnp.concatenate(betas, axis=0))
        return loss

    loss = lax.fori_loop(0, LINES, block, jnp.zeros((8, LANES), f32))
    sum_x[me.x, LINES:LINES + 8, :] = loss


def pull_chunk_of(S, T, w, wide, G):
    def pull_chunk(q, half):
        def rows_block(r, carry):
            rows = aligned(half * HALF + r * 256, 256)
            prod = jnp.dot(w[rows, :], T[q], preferred_element_type=f32)
            gamma = wide[rows, :]
            for side in range(2):
                own = S[2 * q + side, rows, :].astype(f32)
                G[half, 2 * q + side, aligned(r * 256, 256), :] = (
                    gamma * own - prod[:, side * LANES:(side + 1) * LANES]
                )
            return carry

        lax.fori_loop(0, HALF // 256, rows_block, 0)

    return pull_chunk


def reduce_half(me, wire, half, G, out, near_in, far_in, last_near, last_far, pull, spot, line, cross):
    up, down = 1, 3
    front, back = pl.ds(0, QUARTER), pl.ds(QUARTER, QUARTER)
    packed, sent_near, sent_far, last_packed = out

    def add(dst, terms):
        def block(r, carry):
            rows = aligned(r * 256, 256)
            dst[rows, :] = total_of([term[rows, :].astype(f32) for term in terms]).astype(dst.dtype)
            return carry

        lax.fori_loop(0, dst.shape[0] // 256, block, 0)

    def value(t):
        return G.at[half, t]

    pull(2)
    far = []
    for j in range(4):
        add(sent_far.at[j], [value(spot(2, j))])
        far.append((
            wire.start(sent_far.at[j, front], far_in.at[j, 0], line(up)),
            wire.start(sent_far.at[j, back], far_in.at[j, 1], line(down)),
        ))
    yield
    pull(up)
    pull(down)
    near = []
    for j in range(4):
        for way, keep in ((up, 0), (down, 1)):
            far[j][keep].wait_recv()
            chained, direct = (front, back) if keep == 0 else (back, front)
            mine = value(spot(way, j))
            add(sent_near.at[keep, j, chained], [mine.at[chained], far_in.at[j, keep]])
            add(sent_near.at[keep, j, direct], [mine.at[direct]])
            near.append(wire.start(sent_near.at[keep, j], near_in.at[keep, j], line(way)))
    yield
    pull(0)
    for copy in near:
        copy.wait_recv()
    for j in range(4):
        mine = value(spot(0, j))
        add(mine, [mine, near_in.at[0, j], near_in.at[1, j]])
    yield
    here = lambda d: value(spot(0, cross[1](d)))
    add(last_packed.at[2], [here(2)])
    far = (
        wire.start(last_packed.at[2, front], last_far.at[0], cross[0](up)),
        wire.start(last_packed.at[2, back], last_far.at[1], cross[0](down)),
    )
    yield
    near = []
    for way, keep in ((up, 0), (down, 1)):
        far[keep].wait_recv()
        chained, direct = (front, back) if keep == 0 else (back, front)
        mine = here(way)
        add(last_packed.at[keep, chained], [mine.at[chained], last_far.at[keep]])
        add(last_packed.at[keep, direct], [mine.at[direct]])
        near.append(wire.start(last_packed.at[keep], last_near.at[keep], cross[0](way)))
    yield
    for copy in near:
        copy.wait_recv()
    mine = here(0)
    add(mine, [mine, last_near.at[0], last_near.at[1]])
    yield


def kernel(
    band, stu_in, tea_in, grad, stu, tea, loss,
    S, T, z, z_more, w, wide, xsq, ysq, ysq_row,
    row_x, row_z, col_s, sum_x, sum_z, sum_s, shares,
    sent_near, sent_far, last_packed, near_in, far_in, last_near, last_far,
    send, recv,
):
    me = Place()
    barrier = pltpu.get_barrier_semaphore()
    for peer, count in ((me.at_x, 4), (me.at_z, 4), (me.at_s, 8)):
        for d in range(1, count):
            pl.semaphore_signal(barrier, inc=1, device_id=peer(d), device_id_type=MESH)
    pl.semaphore_wait(barrier, 13)
    wire = Wire(send, recv)
    gather(me, wire, stu_in, tea_in, S, T, cost_chunk_of(S, T, z, xsq, ysq))
    finish_cost(me, band, z, xsq, ysq, ysq_row)
    sweeps(me, wire, z, wide, stu, tea, row_x, row_z, col_s)
    make_plan(me, z, wide, tea, xsq, ysq_row, w, sum_x)
    sums = [wire.start(sum_x.at[me.x], sum_x.at[me.x], me.at_x(d)) for d in range(1, 4)]

    pull_chunk = pull_chunk_of(S, T, w, wide, z_more)

    def pull_a(dz):
        row = lax.rem(me.z + dz, 4)
        pull_chunk(2 * row, 0)
        pull_chunk(2 * row + 1, 0)

    pair = lax.div(me.x, 2)

    def pull_b(dx):
        if dx in (2, 0):
            side = 1 - pair if dx == 2 else pair
            for row in range(4):
                pull_chunk(2 * row + side, 1)

    def pull_b_steps(dx):
        if dx == 2:
            pull_b(2)
        elif dx == 1:
            pull_b(0)

    def buffers(half):
        return (None, sent_near.at[half], sent_far.at[half], last_packed.at[half])

    first = reduce_half(
        me, wire, 0, z_more, buffers(0), near_in.at[0], far_in.at[0], last_near.at[0], last_far.at[0],
        pull_a, lambda i, j: lax.rem(me.z + i, 4) * 4 + j, me.at_z,
        (me.at_x, lambda d: lax.rem(me.x + d, 4)),
    )
    second = reduce_half(
        me, wire, 1, z_more, buffers(1), near_in.at[1], far_in.at[1], last_near.at[1], last_far.at[1],
        pull_b_steps, lambda i, j: j * 4 + lax.rem(me.x + i, 4), me.at_x,
        (me.at_z, lambda d: lax.rem(me.z + d, 4)),
    )
    for step in range(6):
        next(first)
        next(second)
        if step == 0:
            for copy in sums:
                copy.wait_recv()
            sum_z[me.z] = total_of([sum_x[i] for i in range(4)])
            sums = [wire.start(sum_z.at[me.z], sum_z.at[me.z], me.at_z(d)) for d in range(1, 4)]
        if step == 1:
            for copy in sums:
                copy.wait_recv()
            summed = total_of([sum_z[i] for i in range(4)])
            stu[...] = stu[...] / kappa
            tea[...] = tea[...] / kappa
            sum_s[me.s] = summed[LINES:, :]
            shares[...] = summed[:LINES, :]
            sums = [wire.start(sum_s.at[me.s], sum_s.at[me.s], me.at_s(d)) for d in range(1, 8)]
            spread_rows(shares, xsq)
        if step == 2:
            for copy in sums:
                copy.wait_recv()
            loss[...] = total_of([sum_s[i] for i in range(8)])
    for half in range(2):
        def block(r, carry):
            here = aligned(r * 256, 256)
            rows = aligned(half * HALF + r * 256, 256)
            grad[rows, :] = xsq[rows, :] * S[me.t, rows, :].astype(f32) + z_more[half, me.t, here, :]
            return carry

        lax.fori_loop(0, HALF // 256, block, 0)
    wire.drain()


def one_device(band_start, student, teacher):
    dma = pltpu.SemaphoreType.DMA
    vmem = pl.BlockSpec(memory_space=pltpu.VMEM)
    scratch = [
        pltpu.VMEM((16, ROWS, LANES), bf16),
        pltpu.VMEM((8, COLS, 256), bf16),
        pltpu.VMEM((TILES, ROWS, LANES), f32),
        pltpu.VMEM((2, 16, HALF, LANES), f32),
        pltpu.VMEM((ROWS, COLS), bf16),
        pltpu.VMEM((ROWS, LANES), f32),
        pltpu.VMEM((ROWS, LANES), f32),
        pltpu.VMEM((COLS, LANES), f32),
        pltpu.VMEM((1, COLS), f32),
        pltpu.VMEM((ITERS, 4, 2, LINES, LANES), f32),
        pltpu.VMEM((ITERS, 4, 2, LINES, LANES), f32),
        pltpu.VMEM((ITERS, 8, 2, COLS), f32),
        pltpu.VMEM((4, LINES + 8, LANES), f32),
        pltpu.VMEM((4, LINES + 8, LANES), f32),
        pltpu.VMEM((8, 8, LANES), f32),
        pltpu.VMEM((LINES, LANES), f32),
        pltpu.VMEM((2, 2, 4, HALF, LANES), bf16),
        pltpu.VMEM((2, 4, HALF, LANES), bf16),
        pltpu.VMEM((2, 3, HALF, LANES), bf16),
        pltpu.VMEM((2, 2, 4, HALF, LANES), bf16),
        pltpu.VMEM((2, 4, 2, QUARTER, LANES), bf16),
        pltpu.VMEM((2, 2, HALF, LANES), bf16),
        pltpu.VMEM((2, 2, QUARTER, LANES), bf16),
        dma((WIRES,)),
        dma((WIRES,)),
    ]
    return pl.pallas_call(
        kernel,
        out_shape=(
            jax.ShapeDtypeStruct((ROWS, LANES), f32),
            jax.ShapeDtypeStruct((LINES, LANES), f32),
            jax.ShapeDtypeStruct((1, COLS), f32),
            jax.ShapeDtypeStruct((8, LANES), f32),
        ),
        in_specs=[pl.BlockSpec(memory_space=pltpu.SMEM), vmem, vmem],
        out_specs=(vmem,) * 4,
        scratch_shapes=scratch,
        compiler_params=pltpu.CompilerParams(
            collective_id=0, has_side_effects=True, vmem_limit_bytes=62 * 2**20
        ),
    )(band_start, student, teacher)


def local(student, teacher, band_start):
    grad, stu, tea, loss = one_device(band_start, student, teacher)
    loss = jnp.sum(loss) * (-1.0 / (kappa * TOKENS))
    return (grad, stu.reshape(ROWS), tea.reshape(COLS), loss)


def solution(mesh):
    placed = (P("stu", "tea"), P("tea", "stu"), P())
    return jax.shard_map(
        local,
        mesh=mesh,
        in_specs=placed,
        out_specs=(P("stu", "tea"), P("stu"), P("tea"), P()),
        check_vma=False,
    )
```

time: 677 us -> 209 us (0.31)
  blocking collectives: 380 us -> 0 us
  Pallas kernels: 0 us -> 198 us
  waiting for transfers between devices: 157 us -> 0 us
  other arithmetic: 113 us -> 1.29 us
  between operations: 14.6 us -> 2.43 us
  local copies, waits for them, and re-layouts: 12.7 us -> 3.54 us
    pallas_call x0 -> x1, Pallas kernels: none -> 198 us  [one_device(): pl.pallas_call(kernel, out_shape=(jax.ShapeDtypeStruct((ROWS, LANES), f32...]
    psum x7 -> x0, blocking collectives: 197 us -> none  [the longest x3 88.2 us: row_logsum(): summed = lax.psum(local_total, 'tea')]
    pmax x6 -> x0, blocking collectives: 182 us -> none  [the longest x3 97.5 us: row_logsum(): highest = lax.pmax(jnp.max(scores, axis=1), 'tea')]
    all_gather x2 -> x0, waiting for transfers between devices: 114 us -> none  [the longest x1 77.2 us: local(): student_full = lax.all_gather(student, 'tea', axis=1, tiled=True)]
    reduce_sum x10 -> x1, other arithmetic: 62 us -> 1.29 us  [local(): loss = jnp.sum(loss) * (-1.0 / (kappa * TOKENS))]
    reduce_scatter x1 -> x0, waiting for transfers between devices: 41.8 us -> none  [local(): lax.psum_scatter(partial_terms, 'tea', scatter_dimension=1, tiled=True)]
    reduce_max x6 -> x0, other arithmetic: 33.9 us -> none  [the longest x3 17.6 us: col_logsum(): highest = lax.pmax(jnp.max(scores, axis=0), 'stu')]
    sub x7 -> x0, other arithmetic: 14 us -> none  [the longest x1 13.9 us: local(): row_mass[:, None] * student_full.astype(jnp.float32) - pulled]
  transfers between devices with their start and end apart: 3 -> 0, of which waited for: 3 -> 0; matrix products, arithmetic and copies ran while one was open for 1% -> 0% of each run, Pallas kernels for 0% -> 0%
where the time goes in v1:
time: 209 us; the launch traced here: 205 us
  Pallas kernels  198 us (95%)
  local copies, waits for them, and re-layouts  3.54 us (2%)
  between operations  2.43 us (1%)
    pallas_call x1, Pallas kernels, one_device(): pl.pallas_call(kernel, out_shape=(jax.ShapeDtypeStruct((ROWS, LANES), f32...  198 us

profile of v1, /device:TPU:1, one launch (start us, length us, event | category | flops | bytes accessed | tf_op | source)
XLA Modules:
  0.0 205.4 jit_solution(10166395919847097704)
XLA Ops:
  0.6 198.2 %shard_map.66 = (f32[2048,128]{1,0:T(8,128)}, f32[16,128]{1,0:T(8,128)}, f32[1,1024]{1,0:T(1,128)}, f32[8,128]{1,0:T(8,128)}) custom-call(s32[32]{0:T(128)} %band.1, bf16[2048,128]{1,0:T(8,128)(2,1)} %stu_in.1, bf16[1024,256]{1,0:T(8,128)(2,1)} %tea_in.1), custom_call_target="tpu_custom_call" | custom-call | tf_op jit(solution)/shard_map/pallas_call | solution.py:581
  198.8 1.3 reduce_sum.9
  200.8 0.0 copy-start
  200.8 2.3 %copy.10 = f32[2048,128]{1,0:T(8,128)} copy(f32[2048,128]{1,0:T(8,128)} %get-tuple-element.16) | data formatting | bytes 2097152
  203.0 0.0 copy-done
  203.0 0.0 copy-start.1
  203.0 0.6 copy.11
  203.6 0.1 copy-done.1
  203.7 0.6 copy.12
Async XLA Ops:
  200.8 2.3 %copy-start = (f32[16,128]{1,0:T(8,128)S(1)}, f32[16,128]{1,0:T(8,128)}, u32[]{:S(2)}) copy-start(f32[16,128]{1,0:T(8,128)} %get-tuple-element.9) | copy-start | bytes 24580
  203.0 0.7 copy-start.1
